TPU v7x, 128 devices: a whole 4x4x4 slice. The times are simulated.
128 devices in a mesh: str: 16 (over x_lo, y, core), crs: 8 (over x_hi, z).
Axes of the slice: x: 4 (x_hi: 2, x_lo: 2; x = x_hi * 2 + x_lo), y: 4, z: 4, core: 2. Of those that a mesh axis runs over, the one named last changes fastest.
Arguments:
- voltage: float32 [4, 512, 16384], P(None, 'str', 'crs'), may hold values from -4 to 0.5
- photocurrent: float32 [4, 512, 16384], P(None, 'str', 'crs'), may hold values from 0.1 to 10
- shunt: float32 [512, 16384], P('str', 'crs'), may hold values from 0.02 to 0.5
- series: float32 [512, 16384], P('str', 'crs'), may hold values from 0.5 to 2
- pattern: int32 [512, 128], P('str', 'crs'), may hold values from 0 to 3
- diode_mask: int32 [512, 128], P('str', 'crs'), may hold values 0 or 1
- aggregate: int32 [512, 128], P('str', 'crs'), may hold values from 0 to 4095, as said below
- coarse_inverse: float32 [4096, 4096], P('crs'), as said below
Outputs:
- newton_step: float32 [4, 512, 16384], P(None, 'str', 'crs')
- residual: float32 [4, 512, 16384], P(None, 'str', 'crs')
Inputs may be any that keep to these rules, and one draw needn't show every extreme that they name: `aggregate`: every value appears. coarse_inverse is symmetric positive definite.
All inputs are finite; a program needn't handle non-finite values. No bound on the sum of `diode_mask` on one device may be relied on, other than what follows from the above.
Results may differ from a plain program's by a relative error of at most 0.0003.
Values sent between devices are 32-bit elements; how exact they have to be, the bound alone decides.
A program may use at most 64 MiB of HBM per device.

v0:
```python
import jax
import jax.numpy as jnp
from jax import lax
from jax.sharding import PartitionSpec as P

ITERS = 3
LEVELS = (0.25, 0.5, 1.0, 2.0)
DIODE_SAT = 0.5


def with_halo(block, sides, width, periodic):
    for axis, dim in sides:
        count = lax.axis_size(axis)
        forward = [(i, i + 1) for i in range(count - 1)]
        if periodic:
            forward.append((count - 1, 0))
        backward = [(target, source) for source, target in forward]
        low = lax.ppermute(
            lax.slice_in_dim(block, block.shape[dim] - width, None, axis=dim), axis, forward
        )
        high = lax.ppermute(lax.slice_in_dim(block, 0, width, axis=dim), axis, backward)
        block = jnp.concatenate([low, block, high], axis=dim)
    return block


def widen(blocks):
    shape = blocks.shape
    spread = jnp.broadcast_to(blocks[..., None], shape + (128,))
    return spread.reshape(shape[:-1] + (shape[-1] * 128,))


def cross_levels(pattern):
    total = jnp.zeros(pattern.shape, jnp.float32)
    for number in range(4):
        total = total + jnp.where(pattern == number, jnp.float32(LEVELS[number]), jnp.float32(0.0))
    return total


def neighbours(field):
    along = with_halo(field, (("str", 1),), 1, True)
    across = with_halo(field, (("crs", 2),), 1, False)
    return (along[:, 2:], along[:, :-2], across[:, :, 2:], across[:, :, :-2])


def shards(voltage, photocurrent, shunt, series, pattern, diode_mask, aggregate, coarse_inverse):
    points = voltage.shape[0]
    rows_here = voltage.shape[1]
    local_block_list = voltage.shape[2] // 128
    coarse_count = coarse_inverse.shape[1]
    cross_level = widen(cross_levels(pattern))
    diode_area = widen(diode_mask.astype(jnp.float32))
    flat_groups = aggregate.reshape(-1)
    stacked = jnp.concatenate([voltage, cross_level[None], series[None]], axis=0)
    below, above, right_cells, left_cells = neighbours(stacked)
    right_link = jnp.minimum(cross_level, right_cells[points])
    left_link = jnp.minimum(cross_level, left_cells[points])
    up_link = above[points + 1]
    diode_derivative = DIODE_SAT * diode_area * jnp.exp(voltage)
    imbalance = (
        shunt * voltage
        + series * (voltage - below[:points])
        + up_link * (voltage - above[:points])
        + right_link * (voltage - right_cells[:points])
        + left_link * (voltage - left_cells[:points])
        + diode_derivative
        - DIODE_SAT * diode_area
        - photocurrent
    )
    diagonal = shunt + diode_derivative + series + up_link + right_link + left_link

    def restrict(remainder):
        block_sums = remainder.reshape(points, rows_here * local_block_list, 128).sum(axis=-1)
        return jax.ops.segment_sum(block_sums.T, flat_groups, num_segments=coarse_count).T

    def interpolate_upward(correction):
        picked = jnp.take(correction, flat_groups, axis=1)
        return widen(picked.reshape(points, rows_here, local_block_list))

    def coarse_solve(incomplete_value):
        product = None
        total = lax.psum(incomplete_value, ("str", "crs"))
        row_share = lax.dot_general(
            total, coarse_inverse, (((1,), (1,)), ((), ())), precision=lax.Precision.HIGHEST
        )
        correction = lax.all_gather(row_share, "crs", axis=1, tiled=True)
        return (correction, product)

    def precondition(remainder):
        resident_portion = remainder / diagonal
        incomplete_value = restrict(remainder)
        correction, product = coarse_solve(incomplete_value)
        smoothed = resident_portion + interpolate_upward(correction)
        product = lax.psum(jnp.sum(remainder * smoothed, axis=(1, 2)), ("str", "crs"))
        return (smoothed, product)

    remainder = -imbalance
    newton_step = jnp.zeros_like(voltage)
    smoothed, product = precondition(remainder)
    direction = smoothed
    for turn in range(ITERS):
        operate_below, operate_above, operate_right_cells, operate_left_cells = neighbours(
            direction
        )
        image = (
            diagonal * direction
            - series * operate_below
            - up_link * operate_above
            - right_link * operate_right_cells
            - left_link * operate_left_cells
        )
        curvature = lax.psum(jnp.sum(direction * image, axis=(1, 2)), ("str", "crs"))
        alpha = (product / curvature)[:, None, None]
        newton_step = newton_step + alpha * direction
        remainder = remainder - alpha * image
        if turn + 1 < ITERS:
            smoothed, fresh = precondition(remainder)
            ratio = (fresh / product)[:, None, None]
            direction = smoothed + ratio * direction
            product = fresh
    return (newton_step, remainder)


def solution(mesh):
    placed = (
        P(None, "str", "crs"),
        P(None, "str", "crs"),
        P("str", "crs"),
        P("str", "crs"),
        P("str", "crs"),
        P("str", "crs"),
        P("str", "crs"),
        P("crs", None),
    )
    return jax.shard_map(
        shards,
        mesh=mesh,
        in_specs=placed,
        out_specs=(P(None, "str", "crs"), P(None, "str", "crs")),
        check_vma=False,
    )
```

profile of v0, /device:TPU:1, one launch (start us, length us, event | category | flops | bytes accessed | tf_op | source)
XLA Modules:
  0.0 1062.8 jit_solution(3380685636923150555)
XLA Ops:
  13.7 4.2 collective-permute-start.3
  20.6 2.9 fusion.30
  26.5 3.8 scatter_custom_fusion
  30.4 158.7 %all-reduce.5.cloned.1.call-done = f32[4,4096]{0,1:T(8,128)} async-done(((f32[4,4096]{0,1:T(8,128)}), f32[4,4096]{0,1:T(8,128)}) %all-reduce.5.cloned.1.call-update) | async-done | bytes 65552 | tf_op jit(solution)/shard_map/psum | solution.py:81
  189.0 10.9 %fusion.54 = f32[4,512]{1,0:T(4,128)S(1)} fusion(f32[4,4096]{0,1:T(8,128)} %all-reduce.5.cloned.1.call-done, f32[512,4096]{1,0:T(8,128)} %param.17), kind=kOutput, calls=%fused_computation.118 | convolution fusion | flops 100663296 | bytes 8462336 | tf_op jit(solution)/shard_map/dot_general | solution.py:82
  199.9 28.1 %all_gather.9 = f32[4,4096]{1,0:T(4,128)S(1)} all-gather(f32[4,512]{1,0:T(4,128)S(1)} %fusion.54), channel_id=1, replica_groups=mesh['str'=16,'crs'=8] {'crs'}, dimensions={1}, use_global_device_ids=true | all-gather | bytes 73728 | tf_op jit(solution)/shard_map/all_gather | solution.py:85
  233.2 2.6 divide_add_fusion.2
  235.8 7.2 collective-permute-start.4
  245.6 4.0 collective-permute-start.7
  252.5 69.2 %all-reduce = (f32[4]{0:T(128)}, f32[4]{0:T(128)}) all-reduce(f32[4]{0:T(128)S(1)} %get-tuple-element.4, f32[4]{0:T(128)S(1)} %get-tuple-element.3), channel_id=1, replica_groups=mesh['str'=16,'crs'=8] {'str','crs'}, use_global_device_ids=true, to_apply=%region_4.6 | all-reduce | flops 8 | bytes 64 | tf_op jit(solution)/shard_map/psum | solution.py:93
  322.4 2.8 multiply_subtract_fusion.2
  327.1 3.8 scatter_custom_fusion.1
  331.1 147.5 %all-reduce.7.cloned.1.call-done = f32[4,4096]{0,1:T(8,128)} async-done(((f32[4,4096]{0,1:T(8,128)}), f32[4,4096]{0,1:T(8,128)}) %all-reduce.7.cloned.1.call-update) | async-done | bytes 65552 | tf_op jit(solution)/shard_map/psum | solution.py:81
  478.6 10.9 %fusion.55 = f32[4,512]{1,0:T(4,128)S(1)} fusion(f32[4,4096]{0,1:T(8,128)} %all-reduce.7.cloned.1.call-done, f32[512,4096]{1,0:T(8,128)} %param.17), kind=kOutput, calls=%fused_computation.119 | convolution fusion | flops 100663296 | bytes 8462336 | tf_op jit(solution)/shard_map/dot_general | solution.py:82
  489.4 27.8 %all_gather.10 = f32[4,4096]{1,0:T(4,128)S(1)} all-gather(f32[4,512]{1,0:T(4,128)S(1)} %fusion.55), channel_id=1, replica_groups=mesh['str'=16,'crs'=8] {'crs'}, dimensions={1}, use_global_device_ids=true | all-gather | bytes 73728 | tf_op jit(solution)/shard_map/all_gather | solution.py:85
  519.2 3.3 gather_fusion.1
  526.9 2.4 reshape.57
  530.8 70.0 %psum.67 = f32[4]{0:T(128)S(1)} all-reduce(f32[4]{0:T(128)S(1)} %multiply_reduce_fusion.3), channel_id=1, replica_groups=mesh['str'=16,'crs'=8] {'str','crs'}, use_global_device_ids=true, to_apply=%region_11.13 | all-reduce | flops 4 | bytes 32 | tf_op jit(solution)/shard_map/psum | solution.py:93
  606.0 4.0 collective-permute-start.11
  613.3 71.4 %psum.68 = f32[4]{0:T(128)} all-reduce(f32[4]{0:T(128)S(1)} %multiply_reduce_fusion.2), channel_id=1, replica_groups=mesh['str'=16,'crs'=8] {'str','crs'}, use_global_device_ids=true, to_apply=%region_13.15 | all-reduce | flops 4 | bytes 32 | tf_op jit(solution)/shard_map/psum | solution.py:111
  685.4 3.1 multiply_subtract_fusion.1
  688.5 2.4 reshape.58
  693.3 4.1 scatter_custom_fusion.2
  697.3 147.4 %all-reduce.9.cloned.1.call-done = f32[4,4096]{0,1:T(8,128)} async-done(((f32[4,4096]{0,1:T(8,128)}), f32[4,4096]{0,1:T(8,128)}) %all-reduce.9.cloned.1.call-update) | async-done | bytes 65552 | tf_op jit(solution)/shard_map/psum | solution.py:81
  844.8 10.9 %fusion.56 = f32[4,512]{1,0:T(4,128)S(1)} fusion(f32[4,4096]{0,1:T(8,128)} %all-reduce.9.cloned.1.call-done, f32[512,4096]{1,0:T(8,128)} %param.17), kind=kOutput, calls=%fused_computation.120 | convolution fusion | flops 100663296 | bytes 8462336 | tf_op jit(solution)/shard_map/dot_general | solution.py:82
  855.6 27.8 %all_gather.11 = f32[4,4096]{1,0:T(4,128)S(1)} all-gather(f32[4,512]{1,0:T(4,128)S(1)} %fusion.56), channel_id=1, replica_groups=mesh['str'=16,'crs'=8] {'crs'}, dimensions={1}, use_global_device_ids=true | all-gather | bytes 73728 | tf_op jit(solution)/shard_map/all_gather | solution.py:85
  885.4 3.2 gather_fusion.2
  893.0 2.4 reshape.59
  897.2 70.1 %psum.70 = f32[4]{0:T(128)S(1)} all-reduce(f32[4]{0:T(128)S(1)} %multiply_reduce_fusion.1), channel_id=1, replica_groups=mesh['str'=16,'crs'=8] {'str','crs'}, use_global_device_ids=true, to_apply=%region_18.20 | all-reduce | flops 4 | bytes 32 | tf_op jit(solution)/shard_map/psum | solution.py:93
  972.6 4.0 collective-permute-start.15
  979.9 71.0 %psum.71 = f32[4]{0:T(128)} all-reduce(f32[4]{0:T(128)S(1)} %multiply_reduce_fusion), channel_id=1, replica_groups=mesh['str'=16,'crs'=8] {'str','crs'}, use_global_device_ids=true, to_apply=%region_20.22 | all-reduce | flops 4 | bytes 32 | tf_op jit(solution)/shard_map/psum | solution.py:111
  1051.6 2.7 multiply_add_fusion
  (176 shorter events, 64.1 us)
Async XLA Ops:
  7.2 181.9 %all-reduce.5.cloned.1.call-start = ((), (), s32[]{:S(2)}) async-start(), calls=%async_computation | async-start | bytes 4194304 | tf_op jit(solution)/shard_map/psum | solution.py:81
  9.5 10.3 collective-permute-start
  11.0 8.6 collective-permute-start.1
  12.4 7.1 collective-permute-start.2
  13.7 5.8 collective-permute-start.3
  30.3 448.3 %all-reduce.7.cloned.1.call-start = ((), (), s32[]{:S(2)}) async-start(), calls=%async_computation.1 | async-start | bytes 4194304 | tf_op jit(solution)/shard_map/psum | solution.py:81
  199.9 30.4 %copy-start.36 = (pred[512]{0:T(512)(128)(4,1)S(1)}, pred[512]{0:T(512)(128)(4,1)}, u32[]{:S(2)}) copy-start(pred[512]{0:T(512)(128)(4,1)} %compare_and_fusion) | copy-start | bytes 1540
  233.2 18.4 %copy-start.4 = (f32[4,32,2048]{2,1,0:T(8,128)S(1)}, f32[4,32,2048]{2,1,0:T(8,128)}, u32[]{:S(2)}) copy-start(f32[4,32,2048]{2,1,0:T(8,128)} %copy-done.3) | copy-start | bytes 3145732
  233.2 18.4 %copy-start.8 = (f32[32,2048]{1,0:T(8,128)S(1)}, f32[32,2048]{1,0:T(8,128)}, u32[]{:S(2)}) copy-start(f32[32,2048]{1,0:T(8,128)} %copy-done.7) | copy-start | bytes 786436
  233.2 18.4 %copy-start.13 = (f32[32,2048]{1,0:T(8,128)S(1)}, f32[32,2048]{1,0:T(8,128)}, u32[]{:S(2)}) copy-start(f32[32,2048]{1,0:T(8,128)} %copy-done.12) | copy-start | bytes 786436
  233.2 18.4 %copy-start.18 = (f32[32,2048]{1,0:T(8,128)S(1)}, f32[32,2048]{1,0:T(8,128)}, u32[]{:S(2)}) copy-start(f32[32,2048]{1,0:T(8,128)} %copy-done.17) | copy-start | bytes 786436
  235.8 15.7 %collective-permute-start.4 = (f32[4,1,2048]{2,1,0:T(1,128)S(1)}, f32[4,1,2048]{2,1,0:T(1,128)S(1)}, u32[]{:S(2)}, u32[]{:S(2)}) collective-permute-start(f32[4,1,2048]{2,1,0:T(1,128)S(1)} %get-tuple-element.24), channel_id=1, source_target_pairs={{8,0},{16,8},{24,16},{32,24},{40,32},{48,40},{56,48},{64,56},{72,6... | collective-permute-start | bytes 98312 | tf_op jit(solution)/shard_map/ppermute | solution.py:21
  243.0 8.6 collective-permute-start.5
  244.3 5.4 collective-permute-start.6
  245.6 5.9 collective-permute-start.7
  251.6 70.8 %copy-start.5 = (f32[4,32,2048]{2,1,0:T(8,128)S(1)}, f32[4,32,2048]{2,1,0:T(8,128)}, u32[]{:S(2)}) copy-start(f32[4,32,2048]{2,1,0:T(8,128)} %copy-done.3) | copy-start | bytes 3145732
  330.9 513.9 %all-reduce.9.cloned.1.call-start = ((), (), s32[]{:S(2)}) async-start(), calls=%async_computation.2 | async-start | bytes 4194304 | tf_op jit(solution)/shard_map/psum | solution.py:81
  529.3 71.5 %copy-start.42 = (f32[4]{0:T(128)S(1)}, f32[4]{0:T(128)}, u32[]{:S(2)}) copy-start(f32[4]{0:T(128)} %get-tuple-element.5) | copy-start | bytes 52
  600.8 11.7 %copy-start.9 = (f32[32,2048]{1,0:T(8,128)S(1)}, f32[32,2048]{1,0:T(8,128)}, u32[]{:S(2)}) copy-start(f32[32,2048]{1,0:T(8,128)} %copy-done.7) | copy-start | bytes 786436
  600.8 11.7 %copy-start.14 = (f32[32,2048]{1,0:T(8,128)S(1)}, f32[32,2048]{1,0:T(8,128)}, u32[]{:S(2)}) copy-start(f32[32,2048]{1,0:T(8,128)} %copy-done.12) | copy-start | bytes 786436
  602.8 8.5 collective-permute-start.8
  604.0 7.3 collective-permute-start.9
  604.7 5.7 collective-permute-start.10
  606.0 5.3 collective-permute-start.11
  895.4 72.0 %copy-start.41 = (f32[4]{0:T(128)S(1)}, f32[4]{0:T(128)}, u32[]{:S(2)}) copy-start(f32[4]{0:T(128)} %copy-done.40) | copy-start | bytes 52
  967.4 11.7 %copy-start.10 = (f32[32,2048]{1,0:T(8,128)S(1)}, f32[32,2048]{1,0:T(8,128)}, u32[]{:S(2)}) copy-start(f32[32,2048]{1,0:T(8,128)} %copy-done.7) | copy-start | bytes 786436
  967.4 11.7 %copy-start.15 = (f32[32,2048]{1,0:T(8,128)S(1)}, f32[32,2048]{1,0:T(8,128)}, u32[]{:S(2)}) copy-start(f32[32,2048]{1,0:T(8,128)} %copy-done.12) | copy-start | bytes 786436
  967.4 11.7 %copy-start.20 = (f32[32,2048]{1,0:T(8,128)S(1)}, f32[32,2048]{1,0:T(8,128)}, u32[]{:S(2)}) copy-start(f32[32,2048]{1,0:T(8,128)} %copy-done.17) | copy-start | bytes 786436
  969.4 8.5 collective-permute-start.12
  970.5 7.3 collective-permute-start.13
  971.3 5.7 collective-permute-start.14
  972.6 5.3 collective-permute-start.15
  (30 other events, 110.5 us)
Sparse Core Ops, SparseCore 0:
  30.4 158.5 all-reduce.4
  331.0 147.5 all-reduce.6
  697.5 147.2 all-reduce.8
where the time goes:
time: 1070 us; the launch traced here: 1060 us
  waiting for transfers between devices  458 us (43%)
  blocking collectives  435 us (41%)
  other arithmetic  50.6 us (5%)
  starting transfers between devices  36.5 us (3%)
  local copies, waits for them, and re-layouts  35 us (3%)
  matrix products  32.6 us (3%)
  between operations  14.5 us (1%)
    psum x3, waiting for transfers between devices, coarse_solve(): total = lax.psum(incomplete_value, ('str', 'crs'))  454 us
    psum x3, blocking collectives, precondition(): lax.psum(jnp.sum(remainder * smoothed, axis=(1, 2)), ('str', 'crs'))  209 us
    psum x2, blocking collectives, shards(): lax.psum(jnp.sum(direction * image, axis=(1, 2)), ('str', 'crs'))  142 us
    all_gather x3, blocking collectives, coarse_solve(): correction = lax.all_gather(row_share, 'crs', axis=1, tiled=True)  83.8 us
    dot_general x3, matrix products, coarse_solve(): lax.dot_general(total, coarse_inverse, (((1,), (1,)), ((), ())), precisio...  32.6 us
  transfers between devices with their start and end apart: 19, of which 9 were waited for; matrix products, arithmetic and copies ran while one was open for 0% of the time, Pallas kernels for 0%

commit v1 on v0

--- a/solution.py
+++ b/solution.py
@@ -78,7 +78,7 @@
 
     def coarse_solve(incomplete_value):
         product = None
-        total = lax.psum(incomplete_value, ("str", "crs"))
+        total = lax.psum(lax.psum(incomplete_value, "str"), "crs")
         row_share = lax.dot_general(
             total, coarse_inverse, (((1,), (1,)), ((), ())), precision=lax.Precision.HIGHEST
         )

time: 1070 us -> 1280 us (1.20)
  waiting for transfers between devices: 458 us -> 650 us
    psum x3 -> x6, waiting for transfers between devices: 454 us -> 646 us  [coarse_solve(): total = lax.psum(lax.psum(incomplete_value, 'str'), 'crs')]
  transfers between devices with their start and end apart: 19 -> 22, of which waited for: 9 -> 10; matrix products, arithmetic and copies ran while one was open for 0% -> 0% of each run, Pallas kernels for 0% -> 0%
where the time goes in v1:
time: 1280 us; the launch traced here: 1270 us
  waiting for transfers between devices  650 us (51%)
  blocking collectives  444 us (35%)
  other arithmetic  50.9 us (4%)
  starting transfers between devices  41.1 us (3%)
  local copies, waits for them, and re-layouts  36 us (3%)
  matrix products  32.6 us (3%)
  between operations  14.9 us (1%)
    psum x6, waiting for transfers between devices, coarse_solve(): total = lax.psum(lax.psum(incomplete_value, 'str'), 'crs')  646 us
    psum x3, blocking collectives, precondition(): lax.psum(jnp.sum(remainder * smoothed, axis=(1, 2)), ('str', 'crs'))  217 us
    psum x2, blocking collectives, shards(): lax.psum(jnp.sum(direction * image, axis=(1, 2)), ('str', 'crs'))  143 us
    all_gather x3, blocking collectives, coarse_solve(): correction = lax.all_gather(row_share, 'crs', axis=1, tiled=True)  84.1 us
    dot_general x3, matrix products, coarse_solve(): lax.dot_general(total, coarse_inverse, (((1,), (1,)), ((), ())), precisio...  32.6 us
  transfers between devices with their start and end apart: 22, of which 10 were waited for; matrix products, arithmetic and copies ran while one was open for 0% of the time, Pallas kernels for 0%

profile of v1, /device:TPU:1, one launch (start us, length us, event | category | flops | bytes accessed | tf_op | source)
XLA Modules:
  0.0 1269.7 jit_solution(911459735426293775)
XLA Ops:
  13.7 4.2 collective-permute-start.3
  20.6 2.9 fusion.30
  26.5 3.6 scatter_custom_fusion
  30.3 130.9 %all-reduce.8.cloned.1.call-done = f32[4,4096]{0,1:T(8,128)} async-done(((f32[4,4096]{0,1:T(8,128)}), f32[4,4096]{0,1:T(8,128)}) %all-reduce.8.cloned.1.call-update) | async-done | bytes 65552 | tf_op jit(solution)/shard_map/psum | solution.py:81
  161.3 91.9 %all-reduce.10.cloned.1.call-done = f32[4,4096]{0,1:T(8,128)} async-done(((f32[4,4096]{0,1:T(8,128)}), f32[4,4096]{0,1:T(8,128)}) %all-reduce.10.cloned.1.call-update) | async-done | bytes 65552 | tf_op jit(solution)/shard_map/psum | solution.py:81
  253.1 10.9 fusion.54
  264.0 28.2 %all_gather.9 = f32[4,4096]{1,0:T(4,128)S(1)} all-gather(f32[4,512]{1,0:T(4,128)S(1)} %fusion.54), channel_id=1, replica_groups=mesh['str'=16,'crs'=8] {'crs'}, dimensions={1}, use_global_device_ids=true | all-gather | bytes 73728 | tf_op jit(solution)/shard_map/all_gather | solution.py:85
  297.3 2.6 divide_add_fusion.2
  299.9 11.7 collective-permute-start.4
  314.2 4.0 collective-permute-start.7
  321.5 69.7 %all-reduce = (f32[4]{0:T(128)}, f32[4]{0:T(128)}) all-reduce(f32[4]{0:T(128)} %get-tuple-element.4, f32[4]{0:T(128)S(1)} %get-tuple-element.3), channel_id=1, replica_groups=mesh['str'=16,'crs'=8] {'str','crs'}, use_global_device_ids=true, to_apply=%region_5.7 | all-reduce | flops 8 | bytes 64 | tf_op jit(solution)/shard_map/psum | solution.py:93
  391.8 2.8 multiply_subtract_fusion.2
  396.5 3.6 scatter_custom_fusion.1
  400.2 119.9 %all-reduce.12.cloned.1.call-done = f32[4,4096]{0,1:T(8,128)} async-done(((f32[4,4096]{0,1:T(8,128)}), f32[4,4096]{0,1:T(8,128)}) %all-reduce.12.cloned.1.call-update) | async-done | bytes 65552 | tf_op jit(solution)/shard_map/psum | solution.py:81
  520.4 91.5 %all-reduce.14.cloned.1.call-done = f32[4,4096]{0,1:T(8,128)} async-done(((f32[4,4096]{0,1:T(8,128)}), f32[4,4096]{0,1:T(8,128)}) %all-reduce.14.cloned.1.call-update) | async-done | bytes 65552 | tf_op jit(solution)/shard_map/psum | solution.py:81
  611.9 10.9 fusion.55
  622.8 28.0 %all_gather.10 = f32[4,4096]{1,0:T(4,128)S(1)} all-gather(f32[4,512]{1,0:T(4,128)S(1)} %fusion.55), channel_id=1, replica_groups=mesh['str'=16,'crs'=8] {'crs'}, dimensions={1}, use_global_device_ids=true | all-gather | bytes 73728 | tf_op jit(solution)/shard_map/all_gather | solution.py:85
  652.7 3.3 gather_fusion.1
  664.4 73.7 %psum.90 = f32[4]{0:T(128)S(1)} all-reduce(f32[4]{0:T(128)S(1)} %multiply_reduce_fusion.3), channel_id=1, replica_groups=mesh['str'=16,'crs'=8] {'str','crs'}, use_global_device_ids=true, to_apply=%region_13.15 | all-reduce | flops 4 | bytes 32 | tf_op jit(solution)/shard_map/psum | solution.py:93
  743.3 4.0 collective-permute-start.11
  751.1 71.5 %psum.91 = f32[4]{0:T(128)} all-reduce(f32[4]{0:T(128)} %multiply_reduce_fusion.2), channel_id=1, replica_groups=mesh['str'=16,'crs'=8] {'str','crs'}, use_global_device_ids=true, to_apply=%region_15.17 | all-reduce | flops 4 | bytes 32 | tf_op jit(solution)/shard_map/psum | solution.py:111
  823.8 3.1 multiply_subtract_fusion.1
  831.7 4.0 scatter_custom_fusion.2
  835.8 119.8 %all-reduce.16.cloned.1.call-done = f32[4,4096]{0,1:T(8,128)} async-done(((f32[4,4096]{0,1:T(8,128)}), f32[4,4096]{0,1:T(8,128)}) %all-reduce.16.cloned.1.call-update) | async-done | bytes 65552 | tf_op jit(solution)/shard_map/psum | solution.py:81
  955.6 91.8 %all-reduce.18.cloned.1.call-done = f32[4,4096]{0,1:T(8,128)} async-done(((f32[4,4096]{0,1:T(8,128)}), f32[4,4096]{0,1:T(8,128)}) %all-reduce.18.cloned.1.call-update) | async-done | bytes 65552 | tf_op jit(solution)/shard_map/psum | solution.py:81
  1047.4 10.9 fusion.56
  1058.3 28.0 %all_gather.11 = f32[4,4096]{1,0:T(4,128)S(1)} all-gather(f32[4,512]{1,0:T(4,128)S(1)} %fusion.56), channel_id=1, replica_groups=mesh['str'=16,'crs'=8] {'crs'}, dimensions={1}, use_global_device_ids=true | all-gather | bytes 73728 | tf_op jit(solution)/shard_map/all_gather | solution.py:85
  1088.2 3.2 gather_fusion.2
  1100.1 73.9 %psum.94 = f32[4]{0:T(128)S(1)} all-reduce(f32[4]{0:T(128)S(1)} %multiply_reduce_fusion.1), channel_id=1, replica_groups=mesh['str'=16,'crs'=8] {'str','crs'}, use_global_device_ids=true, to_apply=%region_21.23 | all-reduce | flops 4 | bytes 32 | tf_op jit(solution)/shard_map/psum | solution.py:93
  1179.1 4.0 collective-permute-start.15
  1186.5 71.1 %psum.95 = f32[4]{0:T(128)} all-reduce(f32[4]{0:T(128)S(1)} %multiply_reduce_fusion), channel_id=1, replica_groups=mesh['str'=16,'crs'=8] {'str','crs'}, use_global_device_ids=true, to_apply=%region_23.25 | all-reduce | flops 4 | bytes 32 | tf_op jit(solution)/shard_map/psum | solution.py:111
  1258.2 2.7 multiply_add_fusion
  (189 shorter events, 72.8 us)
Async XLA Ops:
  7.2 154.0 %all-reduce.8.cloned.1.call-start = ((), (), s32[]{:S(2)}) async-start(), calls=%async_computation | async-start | bytes 4194304 | tf_op jit(solution)/shard_map/psum | solution.py:81
  9.5 10.4 collective-permute-start
  11.0 8.6 collective-permute-start.1
  12.4 7.1 collective-permute-start.2
  13.7 5.8 collective-permute-start.3
  30.2 131.1 %copy-start.38 = (s32[512]{0:T(512)S(1)}, s32[512]{0:T(512)}, u32[]{:S(2)}) copy-start(s32[512]{0:T(512)} %compare_select_fusion) | copy-start | bytes 6148
  30.2 222.9 %all-reduce.10.cloned.1.call-start = ((), (), s32[]{:S(2)}) async-start(), calls=%async_computation.1 | async-start | bytes 4194304 | tf_op jit(solution)/shard_map/psum | solution.py:81
  161.2 358.9 %all-reduce.12.cloned.1.call-start = ((), (), s32[]{:S(2)}) async-start(), calls=%async_computation.2 | async-start | bytes 4194304 | tf_op jit(solution)/shard_map/psum | solution.py:81
  297.3 22.7 %copy-start.4 = (f32[4,32,2048]{2,1,0:T(8,128)S(1)}, f32[4,32,2048]{2,1,0:T(8,128)}, u32[]{:S(2)}) copy-start(f32[4,32,2048]{2,1,0:T(8,128)} %copy-done.3) | copy-start | bytes 3145732
  297.3 22.7 %copy-start.8 = (f32[32,2048]{1,0:T(8,128)S(1)}, f32[32,2048]{1,0:T(8,128)}, u32[]{:S(2)}) copy-start(f32[32,2048]{1,0:T(8,128)} %copy-done.7) | copy-start | bytes 786436
  297.3 22.7 %copy-start.13 = (f32[32,2048]{1,0:T(8,128)S(1)}, f32[32,2048]{1,0:T(8,128)}, u32[]{:S(2)}) copy-start(f32[32,2048]{1,0:T(8,128)} %copy-done.12) | copy-start | bytes 786436
  297.3 22.7 %copy-start.18 = (f32[32,2048]{1,0:T(8,128)S(1)}, f32[32,2048]{1,0:T(8,128)}, u32[]{:S(2)}) copy-start(f32[32,2048]{1,0:T(8,128)} %copy-done.17) | copy-start | bytes 786436
  299.9 20.1 %collective-permute-start.4 = (f32[4,1,2048]{2,1,0:T(1,128)S(1)}, f32[4,1,2048]{2,1,0:T(1,128)S(1)}, u32[]{:S(2)}, u32[]{:S(2)}) collective-permute-start(f32[4,1,2048]{2,1,0:T(1,128)S(1)} %get-tuple-element.24), channel_id=1, source_target_pairs={{8,0},{16,8},{24,16},{32,24},{40,32},{48,40},{56,48},{64,56},{72,6... | collective-permute-start | bytes 98312 | tf_op jit(solution)/shard_map/ppermute | solution.py:21
  311.6 8.4 collective-permute-start.5
  312.9 5.6 collective-permute-start.6
  314.2 5.8 collective-permute-start.7
  320.0 71.8 %copy-start.5 = (f32[4,32,2048]{2,1,0:T(8,128)S(1)}, f32[4,32,2048]{2,1,0:T(8,128)}, u32[]{:S(2)}) copy-start(f32[4,32,2048]{2,1,0:T(8,128)} %copy-done.3) | copy-start | bytes 3145732
  400.2 211.8 %all-reduce.14.cloned.1.call-start = ((), (), s32[]{:S(2)}) async-start(), calls=%async_computation.3 | async-start | bytes 4194304 | tf_op jit(solution)/shard_map/psum | solution.py:81
  520.1 435.4 %all-reduce.16.cloned.1.call-start = ((), (), s32[]{:S(2)}) async-start(), calls=%async_computation.4 | async-start | bytes 4194304 | tf_op jit(solution)/shard_map/psum | solution.py:81
  662.8 75.3 %copy-start.44 = (f32[4]{0:T(128)S(1)}, f32[4]{0:T(128)}, u32[]{:S(2)}) copy-start(f32[4]{0:T(128)} %get-tuple-element.5) | copy-start | bytes 52
  740.1 8.5 collective-permute-start.8
  740.8 7.8 collective-permute-start.9
  742.0 5.3 collective-permute-start.10
  743.3 5.3 collective-permute-start.11
  835.8 211.6 %all-reduce.18.cloned.1.call-start = ((), (), s32[]{:S(2)}) async-start(), calls=%async_computation.5 | async-start | bytes 4194304 | tf_op jit(solution)/shard_map/psum | solution.py:81
  1098.2 75.7 %copy-start.43 = (f32[4]{0:T(128)S(1)}, f32[4]{0:T(128)}, u32[]{:S(2)}) copy-start(f32[4]{0:T(128)} %copy-done.42) | copy-start | bytes 52
  1173.9 11.7 copy-start.15
  1175.9 82.3 %copy-start.41 = (f32[4]{0:T(128)S(1)}, f32[4]{0:T(128)}, u32[]{:S(2)}) copy-start(f32[4]{0:T(128)} %copy-done.40) | copy-start | bytes 52
  1175.9 8.5 collective-permute-start.12
  1176.7 7.8 collective-permute-start.13
  1177.8 5.3 collective-permute-start.14
  1179.1 5.3 collective-permute-start.15
  (35 other events, 157.9 us)
Sparse Core Ops, SparseCore 0:
  30.3 130.7 all-reduce.7
  163.7 89.4 all-reduce.9
  400.3 119.7 all-reduce.11
  522.5 89.4 all-reduce.13
  835.9 119.6 all-reduce.15
  957.9 89.4 all-reduce.17
